TPU v7x, 512 devices: a whole 4x4x16 slice. The times are simulated.
512 devices in a mesh: body: 2 (over core), gx: 16 (over z), gy: 16 (over x, y).
Axes of the slice: x: 4, y: 4, z: 16, core: 2. Of those that a mesh axis runs over, the one named last changes fastest.
Arguments:
- disp: float32 [2, 3, 128, 512, 128], P('body', None, 'gx', 'gy'), may hold values from -4 to 4
- force: float32 [2, 3, 128, 512, 128], P('body', None, 'gx', 'gy'), may hold values from -12 to 12
- kappa: float32 [2, 128, 512, 128], P('body', 'gx', 'gy'), may hold values from 0.05 to 0.5
- sigma: float32 [2, 128, 512, 128], P('body', 'gx', 'gy'), may hold values from 0.2 to 1
- gap0: float32 [512, 128], P(('gx', 'gy')), may hold values from -3 to 3
- pressure: float32 [512, 128], P(('gx', 'gy')), may hold values from 0 to 1
- mortar: float32 [512, 128, 128], P(('gx', 'gy')), may hold values from -0.5 to 0.5
- partner: int32 [512], P(('gx', 'gy')), may hold values from 0 to 31
- active: int32 [512], P(('gx', 'gy')), may hold values 0 or 1
Outputs:
- increment: float32 [2, 3, 128, 512, 128], P('body', None, 'gx', 'gy')
- new_pressure: float32 [512, 128], P(('gx', 'gy'))
Inputs may be any that keep to these rules, and one draw needn't show every extreme that they name: partner numbers a master block of the same gy index: gx index times 2 plus the local block. 1 marks a block of the active contact set.
All inputs are finite; a program needn't handle non-finite values.
Results may differ from a plain program's by a relative error of at most 0.00015.
Values sent between devices are 32-bit elements; how exact they have to be, the bound alone decides.
No kernel may reach another device: no remote copies, remote signals or barrier semaphores. Data moves between devices by JAX's collectives and lax.ppermute only.
A program may use at most 64 MiB of HBM per device.

v0:
```python
import jax
import jax.numpy as jnp
from jax import lax
from jax.sharding import PartitionSpec as P

SBLK = 128
CG_ITERS = 2


def extended(block, sides, width):
    for axis, dim in sides:
        count = lax.axis_size(axis)
        forward = [(i, i + 1) for i in range(count - 1)]
        backward = [(target, source) for source, target in forward]
        low = lax.ppermute(
            lax.slice_in_dim(block, block.shape[dim] - width, None, axis=dim), axis, forward
        )
        high = lax.ppermute(lax.slice_in_dim(block, 0, width, axis=dim), axis, backward)
        block = jnp.concatenate([low, block, high], axis=dim)
    return block


def neighbours():
    result = []
    for first in (-1, 0, 1):
        for second in (-1, 0, 1):
            for third in (-1, 0, 1):
                if first != 0 or second != 0 or third != 0:
                    result.append((first, second, third))
    return result


def apply_stencil(field, padded, kappa, kappa_rim, sigma):
    sizes = field.shape[2:]
    total = sigma[:, None] * field
    for offset in neighbours():
        weight = 0.5 ** (abs(offset[0]) + abs(offset[1]) + abs(offset[2]) - 1)
        lower = [1 + offset[0], 1 + offset[1], 1 + offset[2]]
        bond = 0.5 * (
            kappa
            + kappa_rim[
                :,
                lower[0] : lower[0] + sizes[0],
                lower[1] : lower[1] + sizes[1],
                lower[2] : lower[2] + sizes[2],
            ]
        )
        near = padded[
            :,
            :,
            lower[0] : lower[0] + sizes[0],
            lower[1] : lower[1] + sizes[1],
            lower[2] : lower[2] + sizes[2],
        ]
        total = total + weight * bond[:, None] * (field - near)
    return total


def stencil(field, kappa, kappa_rim, sigma):
    padded = extended(field, (("gx", 2), ("gy", 3)), 1)
    padded = jnp.pad(padded, ((0, 0), (0, 0), (0, 0), (0, 0), (1, 1)))
    return apply_stencil(field, padded, kappa, kappa_rim, sigma)


def gap_of(field, selector, mortar):
    own = field[0, 2, :, :, 0].reshape(1, -1, SBLK)
    rows = lax.all_gather(own, ("body", "gx"), axis=0, tiled=True)
    row_count = lax.axis_size("gx")
    slave_own = lax.dynamic_index_in_dim(rows, lax.axis_index("gx"), 0, keepdims=False)
    master_row = rows[row_count:].reshape(-1, SBLK)
    picked = jnp.dot(selector, master_row, precision=lax.Precision.HIGHEST)
    pulled = jnp.einsum("bij,bj->bi", mortar, picked, precision=lax.Precision.HIGHEST)
    return -slave_own - pulled


def spread(traction, selector, mortar):
    pulled = jnp.einsum("bij,bi->bj", mortar, traction, precision=lax.Precision.HIGHEST)
    row_terms = -jnp.dot(selector.T, pulled, precision=lax.Precision.HIGHEST)
    share = lax.psum_scatter(row_terms, "gx", scatter_dimension=0, tiled=True)
    return jnp.where(lax.axis_index("body") == 0, -traction, share)


def add_surface(image, surface):
    return image.at[0, 2, :, :, 0].add(surface.reshape(image.shape[2], image.shape[3]))


def global_sum(value):
    return lax.psum(value, ("body", "gx", "gy"))


def on_device(disp, force, kappa, sigma, gap0, pressure, mortar, partner, active):
    kappa_rim = extended(kappa, (("gx", 1), ("gy", 2)), 1)
    kappa_rim = jnp.pad(kappa_rim, ((0, 0), (0, 0), (0, 0), (1, 1)))
    row_blocks = mortar.shape[0] * lax.axis_size("gx")
    selector = (partner[:, None] == jnp.arange(row_blocks, dtype=jnp.int32)[None, :]).astype(
        jnp.float32
    )
    flags = active.astype(jnp.float32)[:, None]
    gap = gap0 + gap_of(disp, selector, mortar)
    radius = jnp.sqrt(gap * gap + pressure * pressure + 0.01)
    complement = gap + pressure - radius
    slope_gap = 1.0 - gap / radius
    slope_press = 1.0 - pressure / radius
    divisor = slope_press + 0.5
    stiffness = flags * slope_gap / divisor
    excess = flags * complement / divisor
    rhs = force - stencil(disp, kappa, kappa_rim, sigma)
    rhs = add_surface(rhs, spread(flags * pressure - excess, selector, mortar))
    increment = jnp.zeros_like(rhs)
    residual = rhs
    direction = rhs
    norm_now = global_sum(jnp.sum(residual * residual))
    for step in range(CG_ITERS):
        image = stencil(direction, kappa, kappa_rim, sigma)
        image = add_surface(
            image, spread(stiffness * gap_of(direction, selector, mortar), selector, mortar)
        )
        alpha = norm_now / lax.psum(jnp.sum(direction * image), ("body", "gx", "gy"))
        increment = increment + alpha * direction
        residual = residual - alpha * image
        norm_next = global_sum(jnp.sum(residual * residual))
        direction = residual + norm_next / norm_now * direction
        norm_now = norm_next
    change = gap_of(increment, selector, mortar)
    new_press = flags * (pressure - (complement + slope_gap * change) / divisor)
    return (increment, new_press)


def solution(mesh):
    placed = (
        P("body", None, "gx", "gy", None),
        P("body", None, "gx", "gy", None),
        P("body", "gx", "gy", None),
        P("body", "gx", "gy", None),
        P(("gx", "gy"), None),
        P(("gx", "gy"), None),
        P(("gx", "gy"), None, None),
        P(("gx", "gy")),
        P(("gx", "gy")),
    )
    return jax.shard_map(
        on_device,
        mesh=mesh,
        in_specs=placed,
        out_specs=(P("body", None, "gx", "gy", None), P(("gx", "gy"), None)),
        check_vma=False,
    )
```

profile of v0, /device:TPU:1, one launch (start us, length us, event | category | flops | bytes accessed | tf_op | source)
XLA Modules:
  0.0 782.8 jit_solution(5270657747271295689)
XLA Ops:
  1.5 4.4 collective-permute-start.4
  5.9 1.3 collective-permute-start.5
  7.9 4.2 collective-permute-start
  12.1 1.3 collective-permute-start.1
  13.4 1.0 slice_reduce_fusion.2
  15.2 61.1 %all_gather.12 = f32[32,2,128]{2,1,0:T(2,128)S(1)} all-gather(f32[1,2,128]{2,1,0:T(2,128)S(1)} %reshape_squeeze.12), channel_id=1, replica_groups=mesh['body'=2,'gx'=16,'gy'=16] {'body','gx'}, dimensions={0}, use_global_device_ids=true | all-gather | bytes 33792 | tf_op jit(solution)/shard_map/all_gather | solution.py:67
  79.3 1.3 dynamic-slice.22
  81.3 39.8 %all-reduce.4 = f32[32,128]{1,0:T(8,128)S(1)} all-reduce(f32[32,128]{1,0:T(8,128)S(1)} %convolution_negate_fusion.2), channel_id=2, replica_groups=mesh['body'=2,'gx'=16,'gy'=16] {'gx'}, use_global_device_ids=true, to_apply=%region_0.1.clone | all-reduce | flops 4096 | bytes 32768
  122.0 1.3 collective-permute-start.3
  123.3 4.0 collective-permute-start.2
  129.4 1.3 collective-permute-start.7
  130.7 4.2 collective-permute-start.6
  136.5 2.3 fusion.16
  139.1 1.3 collective-permute-start.9
  140.4 4.0 collective-permute-start.8
  144.5 70.0 %all_gather.13 = f32[32,2,128]{2,1,0:T(2,128)S(1)} all-gather(f32[1,2,128]{2,1,0:T(2,128)S(1)} %reshape_squeeze.13), channel_id=1, replica_groups=mesh['body'=2,'gx'=16,'gy'=16] {'body','gx'}, dimensions={0}, use_global_device_ids=true | all-gather | bytes 33792 | tf_op jit(solution)/shard_map/all_gather | solution.py:67
  216.2 39.1 %all-reduce.5 = f32[32,128]{1,0:T(8,128)S(1)} all-reduce(f32[32,128]{1,0:T(8,128)S(1)} %convolution_negate_fusion.1), channel_id=3, replica_groups=mesh['body'=2,'gx'=16,'gy'=16] {'gx'}, use_global_device_ids=true, to_apply=%region_3.4.clone | all-reduce | flops 4096 | bytes 32768
  255.3 1.3 collective-permute-start.11
  256.6 4.5 collective-permute-start.10
  263.8 2.9 fusion.95
  267.7 125.8 %all-reduce.7 = (f32[]{:T(128)}, f32[]{:T(128)}) all-reduce(f32[]{:T(128)} %get-tuple-element.39, f32[]{:T(128)} %get-tuple-element.38), channel_id=1, replica_groups=mesh['body'=2,'gx'=16,'gy'=16] {'body','gx','gy'}, use_global_device_ids=true, to_apply=%region_2.3 | all-reduce | flops 2 | bytes 16 | tf_op jit(solution)/shard_map/psum | solution.py:88
  395.5 99.7 %psum.30 = f32[]{:T(128)} all-reduce(f32[]{:T(128)} %multiply_reduce_fusion.1), channel_id=1, replica_groups=mesh['body'=2,'gx'=16,'gy'=16] {'body','gx','gy'}, use_global_device_ids=true, to_apply=%region_7.8 | all-reduce | flops 1 | bytes 8 | tf_op jit(solution)/shard_map/psum | solution.py:88
  496.7 1.3 collective-permute-start.13
  498.0 4.0 collective-permute-start.12
  502.1 52.8 %all_gather.14 = f32[32,2,128]{2,1,0:T(2,128)S(1)} all-gather(f32[1,2,128]{2,1,0:T(2,128)S(1)} %reshape_squeeze.14), channel_id=1, replica_groups=mesh['body'=2,'gx'=16,'gy'=16] {'body','gx'}, dimensions={0}, use_global_device_ids=true | all-gather | bytes 33792 | tf_op jit(solution)/shard_map/all_gather | solution.py:67
  557.0 0.9 convolution_negate_fusion
  557.9 39.2 %all-reduce.6 = f32[32,128]{1,0:T(8,128)S(1)} all-reduce(f32[32,128]{1,0:T(8,128)S(1)} %convolution_negate_fusion), channel_id=4, replica_groups=mesh['body'=2,'gx'=16,'gy'=16] {'gx'}, use_global_device_ids=true, to_apply=%region_8.9.clone | all-reduce | flops 4096 | bytes 32768
  597.1 1.3 collective-permute-start.15
  598.4 4.2 collective-permute-start.14
  605.4 2.9 fusion.41
  609.2 117.7 %psum.31 = f32[]{:T(128)} all-reduce(f32[]{:T(128)} %multiply_reduce_fusion), channel_id=1, replica_groups=mesh['body'=2,'gx'=16,'gy'=16] {'body','gx','gy'}, use_global_device_ids=true, to_apply=%region_10.11 | all-reduce | flops 1 | bytes 8 | tf_op jit(solution)/shard_map/psum | solution.py:118
  728.5 53.1 %all_gather.15 = f32[32,2,128]{2,1,0:T(2,128)S(1)} all-gather(f32[1,2,128]{2,1,0:T(2,128)S(1)} %reshape_squeeze.15), channel_id=1, replica_groups=mesh['body'=2,'gx'=16,'gy'=16] {'body','gx'}, dimensions={0}, use_global_device_ids=true | all-gather | bytes 33792 | tf_op jit(solution)/shard_map/all_gather | solution.py:67
  (165 shorter events, 23.4 us)
Async XLA Ops:
  0.6 76.5 %copy-start = (f32[2,128,128]{2,1,0:T(8,128)S(1)}, f32[2,128,128]{2,1,0:T(8,128)}, u32[]{:S(2)}) copy-start(f32[2,128,128]{2,1,0:T(8,128)} %param.21) | copy-start | bytes 393220
  0.6 127.6 %copy-start.26 = (f32[1,8,32,128]{3,2,1,0:T(8,128)S(1)}, f32[1,8,32,128]{3,2,1,0:T(8,128)}, u32[]{:S(2)}) copy-start(f32[1,8,32,128]{3,2,1,0:T(8,128)} %param.17) | copy-start | bytes 393220
  1.5 127.2 %collective-permute-start.4 = (f32[1,3,1,32,128]{4,3,2,1,0:T(8,128)S(1)}, f32[1,3,1,32,128]{4,3,2,1,0:T(8,128)S(1)}, u32[]{:S(2)}, u32[]{:S(2)}) collective-permute-start(f32[1,3,1,32,128]{4,3,2,1,0:T(8,128)S(1)} %get-tuple-element.82), channel_id=1, source_target_pairs={{0,16},{16,32},{32,48},{48,64},{64,80},{80,96},{96,112},{112,128},... | collective-permute-start | bytes 147464 | tf_op jit(solution)/shard_map/ppermute | solution.py:15
  5.9 123.4 %collective-permute-start.5 = (f32[1,3,1,32,128]{4,3,2,1,0:T(8,128)S(1)}, f32[1,3,1,32,128]{4,3,2,1,0:T(8,128)S(1)}, u32[]{:S(2)}, u32[]{:S(2)}) collective-permute-start(f32[1,3,1,32,128]{4,3,2,1,0:T(8,128)S(1)} %get-tuple-element.81), channel_id=1, source_target_pairs={{16,0},{32,16},{48,32},{64,48},{80,64},{96,80},{112,96},{128,112},... | collective-permute-start | bytes 147464 | tf_op jit(solution)/shard_map/ppermute | solution.py:18
  7.9 113.1 %collective-permute-start = (f32[1,1,32,128]{3,2,1,0:T(8,128)S(1)}, f32[1,1,32,128]{3,2,1,0:T(8,128)S(1)}, u32[]{:S(2)}, u32[]{:S(2)}) collective-permute-start(f32[1,1,32,128]{3,2,1,0:T(8,128)S(1)} %get-tuple-element.97), channel_id=1, source_target_pairs={{0,16},{16,32},{32,48},{48,64},{64,80},{80,96},{96,112},{112,128},... | collective-permute-start | bytes 49160 | tf_op jit(solution)/shard_map/ppermute | solution.py:15
  12.1 109.8 %collective-permute-start.1 = (f32[1,1,32,128]{3,2,1,0:T(8,128)S(1)}, f32[1,1,32,128]{3,2,1,0:T(8,128)S(1)}, u32[]{:S(2)}, u32[]{:S(2)}) collective-permute-start(f32[1,1,32,128]{3,2,1,0:T(8,128)S(1)} %get-tuple-element.96), channel_id=1, source_target_pairs={{16,0},{32,16},{48,32},{64,48},{80,64},{96,80},{112,96},{128,112},... | collective-permute-start | bytes 49160 | tf_op jit(solution)/shard_map/ppermute | solution.py:18
  122.0 5.5 collective-permute-start.3
  123.3 4.7 collective-permute-start.2
  128.8 134.0 %copy-start.2 = (f32[8,32,128]{2,1,0:T(8,128)}, f32[8,32,128]{2,1,0:T(8,128)S(1)}, u32[]{:S(2)}) copy-start(f32[8,32,128]{2,1,0:T(8,128)S(1)} %get-tuple-element.66) | copy-start | bytes 393220
  129.4 5.8 collective-permute-start.7
  130.7 5.1 collective-permute-start.6
  135.0 3.8 copy-start.8
  135.0 3.8 copy-start.11
  135.1 3.7 copy-start.14
  135.1 127.6 %copy-start.4 = (f32[8,32,128]{2,1,0:T(8,128)}, f32[8,32,128]{2,1,0:T(8,128)S(1)}, u32[]{:S(2)}) copy-start(f32[8,32,128]{2,1,0:T(8,128)S(1)} %get-tuple-element.83) | copy-start | bytes 393220
  135.1 127.6 %copy-start.6 = (f32[8,32,128]{2,1,0:T(8,128)}, f32[8,32,128]{2,1,0:T(8,128)S(1)}, u32[]{:S(2)}) copy-start(f32[8,32,128]{2,1,0:T(8,128)S(1)} %get-tuple-element.84) | copy-start | bytes 393220
  136.5 78.0 %copy-start.39 = (s32[2]{0:T(128)S(1)}, s32[2]{0:T(128)}, u32[]{:S(2)}) copy-start(s32[2]{0:T(128)} %param.22) | copy-start | bytes 28
  136.5 78.5 %copy-start.38 = (f32[2,128]{1,0:T(2,128)S(1)}, f32[2,128]{1,0:T(2,128)}, u32[]{:S(2)}) copy-start(f32[2,128]{1,0:T(2,128)} %param.20) | copy-start | bytes 3076
  139.1 116.1 %collective-permute-start.9 = (f32[1,3,1,32,128]{4,3,2,1,0:T(8,128)S(1)}, f32[1,3,1,32,128]{4,3,2,1,0:T(8,128)S(1)}, u32[]{:S(2)}, u32[]{:S(2)}) collective-permute-start(f32[1,3,1,32,128]{4,3,2,1,0:T(8,128)S(1)} %get-tuple-element.80), channel_id=1, source_target_pairs={{16,0},{32,16},{48,32},{64,48},{80,64},{96,80},{112,96},{128,112},... | collective-permute-start | bytes 147464 | tf_op jit(solution)/shard_map/ppermute | solution.py:18
  140.4 114.8 %collective-permute-start.8 = (f32[1,3,1,32,128]{4,3,2,1,0:T(8,128)S(1)}, f32[1,3,1,32,128]{4,3,2,1,0:T(8,128)S(1)}, u32[]{:S(2)}, u32[]{:S(2)}) collective-permute-start(f32[1,3,1,32,128]{4,3,2,1,0:T(8,128)S(1)} %get-tuple-element.79), channel_id=1, source_target_pairs={{0,16},{16,32},{32,48},{48,64},{64,80},{80,96},{96,112},{112,128},... | collective-permute-start | bytes 147464 | tf_op jit(solution)/shard_map/ppermute | solution.py:15
  255.2 7.5 copy-start.32
  255.2 7.5 copy-start.33
  255.3 6.7 collective-permute-start.11
  256.6 5.4 collective-permute-start.10
  496.7 100.4 %collective-permute-start.13 = (f32[1,3,1,32,128]{4,3,2,1,0:T(8,128)S(1)}, f32[1,3,1,32,128]{4,3,2,1,0:T(8,128)S(1)}, u32[]{:S(2)}, u32[]{:S(2)}) collective-permute-start(f32[1,3,1,32,128]{4,3,2,1,0:T(8,128)S(1)} %get-tuple-element.78), channel_id=1, source_target_pairs={{16,0},{32,16},{48,32},{64,48},{80,64},{96,80},{112,96},{128,112},... | collective-permute-start | bytes 147464 | tf_op jit(solution)/shard_map/ppermute | solution.py:18
  498.0 99.1 %collective-permute-start.12 = (f32[1,3,1,32,128]{4,3,2,1,0:T(8,128)S(1)}, f32[1,3,1,32,128]{4,3,2,1,0:T(8,128)S(1)}, u32[]{:S(2)}, u32[]{:S(2)}) collective-permute-start(f32[1,3,1,32,128]{4,3,2,1,0:T(8,128)S(1)} %get-tuple-element.77), channel_id=1, source_target_pairs={{0,16},{16,32},{32,48},{48,64},{64,80},{80,96},{96,112},{112,128},... | collective-permute-start | bytes 147464 | tf_op jit(solution)/shard_map/ppermute | solution.py:15
  597.1 7.1 copy-start.30
  597.1 7.1 copy-start.31
  597.1 6.4 collective-permute-start.15
  598.4 5.1 collective-permute-start.14
  608.3 173.3 %copy-start.40 = (s32[2]{0:T(128)S(1)}, s32[2]{0:T(128)}, u32[]{:S(2)}) copy-start(s32[2]{0:T(128)} %param.22) | copy-start | bytes 28
  728.3 54.5 %copy-start.34 = (f32[1,3,8,32,128]{4,3,2,1,0:T(8,128)}, f32[1,3,8,32,128]{4,3,2,1,0:T(8,128)S(1)}, u32[]{:S(2)}) copy-start(f32[1,3,8,32,128]{4,3,2,1,0:T(8,128)S(1)} %multiply_add_fusion) | copy-start | bytes 1179652
  (25 other events, 39.2 us)
where the time goes:
time: 784 us; the launch traced here: 783 us
  blocking collectives  698 us (89%)
  starting transfers between devices  43.8 us (6%)
  other arithmetic  16.7 us (2%)
  local copies, waits for them, and re-layouts  10.8 us (1%)
    all_gather x4, blocking collectives, gap_of(): rows = lax.all_gather(own, ('body', 'gx'), axis=0, tiled=True)  237 us
    psum x2, blocking collectives, global_sum(): return lax.psum(value, ('body', 'gx', 'gy'))  226 us
    unnamed x3, blocking collectives  118 us
    psum x1, blocking collectives, on_device(): lax.psum(jnp.sum(direction * image), ('body', 'gx', 'gy'))  118 us
    ppermute x8, starting transfers between devices, extended(): lax.ppermute(lax.slice_in_dim(block, block.shape[dim] - width, None, axis...  33.4 us
  transfers between devices with their start and end apart: 16, of which 2 were waited for; matrix products, arithmetic and copies ran while one was open for 2% of the time, Pallas kernels for 0%

commit v1 on v0

--- a/solution.py
+++ b/solution.py
@@ -64,7 +64,10 @@
 
 def gap_of(field, selector, mortar):
     own = field[0, 2, :, :, 0].reshape(1, -1, SBLK)
-    rows = lax.all_gather(own, ("body", "gx"), axis=0, tiled=True)
+    rows = jnp.concatenate(
+        lax.all_to_all(jnp.stack([own] * lax.axis_size(("body", "gx"))), ("body", "gx"), 0, 0),
+        axis=0,
+    )
     row_count = lax.axis_size("gx")
     slave_own = lax.dynamic_index_in_dim(rows, lax.axis_index("gx"), 0, keepdims=False)
     master_row = rows[row_count:].reshape(-1, SBLK)

time: 784 us -> 644 us (0.82)
  blocking collectives: 698 us -> 475 us
  starting transfers between devices: 43.8 us -> 99.2 us
  waiting for transfers between devices: 1.14 us -> 21.9 us
    all_gather x4 -> x0, blocking collectives: 237 us -> none  [gap_of(): rows = lax.all_gather(own, ('body', 'gx'), axis=0, tiled=True)]
    all_to_all x0 -> x3, starting transfers between devices: none -> 56.9 us  [gap_of(): lax.all_to_all(jnp.stack([own] * lax.axis_size(('body', 'gx'))), ('body',...]
    all_to_all x0 -> x1, blocking collectives: none -> 19.4 us  [gap_of(): lax.all_to_all(jnp.stack([own] * lax.axis_size(('body', 'gx'))), ('body',...]
    all_to_all x0 -> x3, waiting for transfers between devices: none -> 15.5 us  [gap_of(): lax.all_to_all(jnp.stack([own] * lax.axis_size(('body', 'gx'))), ('body',...]
  transfers between devices with their start and end apart: 16 -> 19, of which waited for: 2 -> 6; matrix products, arithmetic and copies ran while one was open for 2% -> 3% of each run, Pallas kernels for 0% -> 0%
where the time goes in v1:
time: 644 us; the launch traced here: 642 us
  blocking collectives  475 us (74%)
  starting transfers between devices  99.2 us (15%)
  waiting for transfers between devices  21.9 us (3%)
  other arithmetic  18.6 us (3%)
  local copies, waits for them, and re-layouts  14.7 us (2%)
  matrix products  6.7 us (1%)
  between operations  6.52 us (1%)
    psum x2, blocking collectives, global_sum(): return lax.psum(value, ('body', 'gx', 'gy'))  220 us
    unnamed x3, blocking collectives  121 us
    psum x1, blocking collectives, on_device(): lax.psum(jnp.sum(direction * image), ('body', 'gx', 'gy'))  114 us
    all_to_all x3, starting transfers between devices, gap_of(): lax.all_to_all(jnp.stack([own] * lax.axis_size(('body', 'gx'))), ('body',...  56.9 us
    ppermute x8, starting transfers between devices, extended(): lax.ppermute(lax.slice_in_dim(block, block.shape[dim] - width, None, axis...  31.9 us
    all_to_all x1, blocking collectives, gap_of(): lax.all_to_all(jnp.stack([own] * lax.axis_size(('body', 'gx'))), ('body',...  19.4 us
    all_to_all x3, waiting for transfers between devices, gap_of(): lax.all_to_all(jnp.stack([own] * lax.axis_size(('body', 'gx'))), ('body',...  15.5 us
  transfers between devices with their start and end apart: 19, of which 6 were waited for; matrix products, arithmetic and copies ran while one was open for 3% of the time, Pallas kernels for 0%

profile of v1, /device:TPU:1, one launch (start us, length us, event | category | flops | bytes accessed | tf_op | source)
XLA Modules:
  0.0 642.3 jit_solution(15906893632857885120)
XLA Ops:
  1.4 4.4 collective-permute-start
  6.7 3.5 collective-permute-start.4
  10.2 1.3 collective-permute-start.5
  11.5 1.3 collective-permute-start.1
  13.7 3.5 collective-permute-done.1
  17.3 1.3 collective-permute-start.3
  18.6 4.0 collective-permute-start.2
  24.3 18.0 %all-to-all-start = ((f32[32,1,2,128]{3,2,1,0:T(2,128)}), f32[32,1,2,128]{3,2,1,0:T(2,128)}, u32[]{:S(2)}, u32[]{:S(2)}) async-start(f32[32,1,2,128]{3,2,1,0:T(2,128)} %stack.12), calls=%async_computation | async-start | bytes 65536 | tf_op jit(solution)/shard_map/all_to_all | solution.py:68
  43.5 1.3 dynamic-slice.26
  48.0 1.3 collective-permute-start.7
  49.3 4.0 collective-permute-start.6
  54.9 3.1 fusion.16
  61.2 42.5 %all-reduce.4 = f32[32,128]{1,0:T(8,128)S(1)} all-reduce(f32[32,128]{1,0:T(8,128)S(1)} %convolution_negate_fusion.2), channel_id=2, replica_groups=mesh['body'=2,'gx'=16,'gy'=16] {'gx'}, use_global_device_ids=true, to_apply=%region_0.1.clone | all-reduce | flops 4096 | bytes 32768
  104.2 1.3 collective-permute-start.9
  105.5 4.0 collective-permute-start.8
  110.7 1.3 collective-permute-start.11
  112.0 4.1 collective-permute-start.10
  116.8 27.5 %all-to-all-start.1 = ((f32[32,1,2,128]{3,2,1,0:T(2,128)}), f32[32,1,2,128]{3,2,1,0:T(2,128)}, u32[]{:S(2)}, u32[]{:S(2)}) async-start(f32[32,1,2,128]{3,2,1,0:T(2,128)} %stack.13), calls=%async_computation.1 | async-start | bytes 65536 | tf_op jit(solution)/shard_map/all_to_all | solution.py:68
  146.1 2.9 fusion.95
  149.0 7.8 %all-to-all-done.1 = f32[32,1,2,128]{3,2,1,0:T(2,128)} async-done(((f32[32,1,2,128]{3,2,1,0:T(2,128)}), f32[32,1,2,128]{3,2,1,0:T(2,128)}, u32[]{:S(2)}, u32[]{:S(2)}) %all-to-all-start.1) | async-done | bytes 32800 | tf_op jit(solution)/shard_map/all_to_all | solution.py:68
  158.7 1.3 fusion.243
  161.1 39.4 %all-reduce.5 = f32[32,128]{1,0:T(8,128)S(1)} all-reduce(f32[32,128]{1,0:T(8,128)S(1)} %convolution_negate_fusion.1), channel_id=3, replica_groups=mesh['body'=2,'gx'=16,'gy'=16] {'gx'}, use_global_device_ids=true, to_apply=%region_3.4.clone | all-reduce | flops 4096 | bytes 32768
  201.7 120.5 %all-reduce.7 = (f32[]{:T(128)}, f32[]{:T(128)}) all-reduce(f32[]{:T(128)} %get-tuple-element.39, f32[]{:T(128)} %get-tuple-element.38), channel_id=1, replica_groups=mesh['body'=2,'gx'=16,'gy'=16] {'body','gx','gy'}, use_global_device_ids=true, to_apply=%region_2.3 | all-reduce | flops 2 | bytes 16 | tf_op jit(solution)/shard_map/psum | solution.py:91
  324.4 99.7 %psum.30 = f32[]{:T(128)} all-reduce(f32[]{:T(128)} %multiply_reduce_fusion.1), channel_id=1, replica_groups=mesh['body'=2,'gx'=16,'gy'=16] {'body','gx','gy'}, use_global_device_ids=true, to_apply=%region_7.8 | all-reduce | flops 1 | bytes 8 | tf_op jit(solution)/shard_map/psum | solution.py:91
  426.8 4.0 collective-permute-start.12
  433.3 4.0 collective-permute-start.14
  438.1 11.4 %all-to-all-start.2 = ((f32[32,1,2,128]{3,2,1,0:T(2,128)}), f32[32,1,2,128]{3,2,1,0:T(2,128)}, u32[]{:S(2)}, u32[]{:S(2)}) async-start(f32[32,1,2,128]{3,2,1,0:T(2,128)} %stack.14), calls=%async_computation.2 | async-start | bytes 65536 | tf_op jit(solution)/shard_map/all_to_all | solution.py:68
  451.5 2.9 fusion.41
  454.4 7.7 %all-to-all-done.2 = f32[32,1,2,128]{3,2,1,0:T(2,128)} async-done(((f32[32,1,2,128]{3,2,1,0:T(2,128)}), f32[32,1,2,128]{3,2,1,0:T(2,128)}, u32[]{:S(2)}, u32[]{:S(2)}) %all-to-all-start.2) | async-done | bytes 32800 | tf_op jit(solution)/shard_map/all_to_all | solution.py:68
  465.7 39.4 %all-reduce.6 = f32[32,128]{1,0:T(8,128)S(1)} all-reduce(f32[32,128]{1,0:T(8,128)S(1)} %convolution_negate_fusion), channel_id=4, replica_groups=mesh['body'=2,'gx'=16,'gy'=16] {'gx'}, use_global_device_ids=true, to_apply=%region_8.9.clone | all-reduce | flops 4096 | bytes 32768
  506.3 113.8 %psum.31 = f32[]{:T(128)} all-reduce(f32[]{:T(128)} %multiply_reduce_fusion), channel_id=1, replica_groups=mesh['body'=2,'gx'=16,'gy'=16] {'body','gx','gy'}, use_global_device_ids=true, to_apply=%region_10.11 | all-reduce | flops 1 | bytes 8 | tf_op jit(solution)/shard_map/psum | solution.py:121
  621.7 19.4 %all_to_all.20 = f32[32,1,2,128]{3,2,1,0:T(2,128)S(1)} all-to-all(f32[32,1,2,128]{3,2,1,0:T(2,128)S(1)} %stack.15), channel_id=1, replica_groups=mesh['body'=2,'gx'=16,'gy'=16] {'body','gx'}, dimensions={0} | all-to-all | bytes 65536 | tf_op jit(solution)/shard_map/all_to_all | solution.py:68
  (186 shorter events, 34.0 us)
Async XLA Ops:
  0.6 58.3 %copy-start = (f32[2,128,128]{2,1,0:T(8,128)S(1)}, f32[2,128,128]{2,1,0:T(8,128)}, u32[]{:S(2)}) copy-start(f32[2,128,128]{2,1,0:T(8,128)} %param.21) | copy-start | bytes 393220
  0.6 46.3 %copy-start.26 = (f32[1,8,32,128]{3,2,1,0:T(8,128)S(1)}, f32[1,8,32,128]{3,2,1,0:T(8,128)}, u32[]{:S(2)}) copy-start(f32[1,8,32,128]{3,2,1,0:T(8,128)} %param.17) | copy-start | bytes 393220
  1.4 11.4 %collective-permute-start = (f32[1,1,32,128]{3,2,1,0:T(8,128)S(1)}, f32[1,1,32,128]{3,2,1,0:T(8,128)S(1)}, u32[]{:S(2)}, u32[]{:S(2)}) collective-permute-start(f32[1,1,32,128]{3,2,1,0:T(8,128)S(1)} %get-tuple-element.97), channel_id=1, source_target_pairs={{0,16},{16,32},{32,48},{48,64},{64,80},{80,96},{96,112},{112,128},... | collective-permute-start | bytes 49160 | tf_op jit(solution)/shard_map/ppermute | solution.py:15
  6.7 40.8 %collective-permute-start.4 = (f32[1,3,1,32,128]{4,3,2,1,0:T(8,128)S(1)}, f32[1,3,1,32,128]{4,3,2,1,0:T(8,128)S(1)}, u32[]{:S(2)}, u32[]{:S(2)}) collective-permute-start(f32[1,3,1,32,128]{4,3,2,1,0:T(8,128)S(1)} %get-tuple-element.82), channel_id=1, source_target_pairs={{0,16},{16,32},{32,48},{48,64},{64,80},{80,96},{96,112},{112,128},... | collective-permute-start | bytes 147464 | tf_op jit(solution)/shard_map/ppermute | solution.py:15
  10.2 37.7 %collective-permute-start.5 = (f32[1,3,1,32,128]{4,3,2,1,0:T(8,128)S(1)}, f32[1,3,1,32,128]{4,3,2,1,0:T(8,128)S(1)}, u32[]{:S(2)}, u32[]{:S(2)}) collective-permute-start(f32[1,3,1,32,128]{4,3,2,1,0:T(8,128)S(1)} %get-tuple-element.81), channel_id=1, source_target_pairs={{16,0},{32,16},{48,32},{64,48},{80,64},{96,80},{112,96},{128,112},... | collective-permute-start | bytes 147464 | tf_op jit(solution)/shard_map/ppermute | solution.py:18
  11.5 5.8 collective-permute-start.1
  17.3 28.3 %copy-start.38 = (f32[1,1,32,128]{3,2,1,0:T(8,128)}, f32[1,1,32,128]{3,2,1,0:T(8,128)S(1)}, u32[]{:S(2)}) copy-start(f32[1,1,32,128]{3,2,1,0:T(8,128)S(1)} %collective-permute-done.1) | copy-start | bytes 49156
  17.3 28.2 %collective-permute-start.3 = (f32[1,10,1,128]{3,2,1,0:T(1,128)S(1)}, f32[1,10,1,128]{3,2,1,0:T(1,128)S(1)}, u32[]{:S(2)}, u32[]{:S(2)}) collective-permute-start(f32[1,10,1,128]{3,2,1,0:T(1,128)S(1)} %get-tuple-element.93), channel_id=1, source_target_pairs={{1,0},{2,1},{3,2},{4,3},{5,4},{6,5},{7,6},{8,7},{9,8},{10,9},{11,1... | collective-permute-start | bytes 15368 | tf_op jit(solution)/shard_map/ppermute | solution.py:18
  18.6 26.9 %collective-permute-start.2 = (f32[1,10,1,128]{3,2,1,0:T(1,128)S(1)}, f32[1,10,1,128]{3,2,1,0:T(1,128)S(1)}, u32[]{:S(2)}, u32[]{:S(2)}) collective-permute-start(f32[1,10,1,128]{3,2,1,0:T(1,128)S(1)} %get-tuple-element.92), channel_id=1, source_target_pairs={{0,1},{1,2},{2,3},{3,4},{4,5},{5,6},{6,7},{7,8},{8,9},{9,10},{10,1... | collective-permute-start | bytes 15368 | tf_op jit(solution)/shard_map/ppermute | solution.py:15
  24.3 33.8 %all-to-all-start = ((f32[32,1,2,128]{3,2,1,0:T(2,128)}), f32[32,1,2,128]{3,2,1,0:T(2,128)}, u32[]{:S(2)}, u32[]{:S(2)}) async-start(f32[32,1,2,128]{3,2,1,0:T(2,128)} %stack.12), calls=%async_computation | async-start | bytes 65536 | tf_op jit(solution)/shard_map/all_to_all | solution.py:68
  47.4 97.6 %copy-start.2 = (f32[8,32,128]{2,1,0:T(8,128)}, f32[8,32,128]{2,1,0:T(8,128)S(1)}, u32[]{:S(2)}) copy-start(f32[8,32,128]{2,1,0:T(8,128)S(1)} %get-tuple-element.66) | copy-start | bytes 393220
  47.4 7.2 %copy-start.36 = (f32[1,3,1,32,128]{4,3,2,1,0:T(8,128)}, f32[1,3,1,32,128]{4,3,2,1,0:T(8,128)S(1)}, u32[]{:S(2)}) copy-start(f32[1,3,1,32,128]{4,3,2,1,0:T(8,128)S(1)} %collective-permute-done.4) | copy-start | bytes 147460
  48.0 5.6 collective-permute-start.7
  49.3 4.8 collective-permute-start.6
  53.5 91.6 %copy-start.4 = (f32[8,32,128]{2,1,0:T(8,128)}, f32[8,32,128]{2,1,0:T(8,128)S(1)}, u32[]{:S(2)}) copy-start(f32[8,32,128]{2,1,0:T(8,128)S(1)} %get-tuple-element.83) | copy-start | bytes 393220
  53.5 91.6 %copy-start.6 = (f32[8,32,128]{2,1,0:T(8,128)}, f32[8,32,128]{2,1,0:T(8,128)S(1)}, u32[]{:S(2)}) copy-start(f32[8,32,128]{2,1,0:T(8,128)S(1)} %get-tuple-element.84) | copy-start | bytes 393220
  104.2 5.3 collective-permute-start.9
  105.5 5.2 collective-permute-start.8
  109.5 35.5 %copy-start.32 = (f32[1,3,1,32,128]{4,3,2,1,0:T(8,128)}, f32[1,3,1,32,128]{4,3,2,1,0:T(8,128)S(1)}, u32[]{:S(2)}) copy-start(f32[1,3,1,32,128]{4,3,2,1,0:T(8,128)S(1)} %collective-permute-done.9) | copy-start | bytes 147460
  110.7 34.4 %copy-start.33 = (f32[1,3,1,32,128]{4,3,2,1,0:T(8,128)}, f32[1,3,1,32,128]{4,3,2,1,0:T(8,128)S(1)}, u32[]{:S(2)}) copy-start(f32[1,3,1,32,128]{4,3,2,1,0:T(8,128)S(1)} %collective-permute-done.8) | copy-start | bytes 147460
  110.7 33.6 %collective-permute-start.11 = (f32[1,3,10,1,128]{4,3,2,1,0:T(1,128)S(1)}, f32[1,3,10,1,128]{4,3,2,1,0:T(1,128)S(1)}, u32[]{:S(2)}, u32[]{:S(2)}) collective-permute-start(f32[1,3,10,1,128]{4,3,2,1,0:T(1,128)S(1)} %get-tuple-element.74), channel_id=1, source_target_pairs={{1,0},{2,1},{3,2},{4,3},{5,4},{6,5},{7,6},{8,7},{9,8},{10,9},{11,1... | collective-permute-start | bytes 46088 | tf_op jit(solution)/shard_map/ppermute | solution.py:18
  112.0 32.3 %collective-permute-start.10 = (f32[1,3,10,1,128]{4,3,2,1,0:T(1,128)S(1)}, f32[1,3,10,1,128]{4,3,2,1,0:T(1,128)S(1)}, u32[]{:S(2)}, u32[]{:S(2)}) collective-permute-start(f32[1,3,10,1,128]{4,3,2,1,0:T(1,128)S(1)} %get-tuple-element.73), channel_id=1, source_target_pairs={{0,1},{1,2},{2,3},{3,4},{4,5},{5,6},{6,7},{7,8},{8,9},{9,10},{10,1... | collective-permute-start | bytes 46088 | tf_op jit(solution)/shard_map/ppermute | solution.py:15
  116.8 40.0 %all-to-all-start.1 = ((f32[32,1,2,128]{3,2,1,0:T(2,128)}), f32[32,1,2,128]{3,2,1,0:T(2,128)}, u32[]{:S(2)}, u32[]{:S(2)}) async-start(f32[32,1,2,128]{3,2,1,0:T(2,128)} %stack.13), calls=%async_computation.1 | async-start | bytes 65536 | tf_op jit(solution)/shard_map/all_to_all | solution.py:68
  425.5 5.3 collective-permute-start.13
  426.8 5.2 collective-permute-start.12
  430.8 19.2 %copy-start.30 = (f32[1,3,1,32,128]{4,3,2,1,0:T(8,128)}, f32[1,3,1,32,128]{4,3,2,1,0:T(8,128)S(1)}, u32[]{:S(2)}) copy-start(f32[1,3,1,32,128]{4,3,2,1,0:T(8,128)S(1)} %collective-permute-done.13) | copy-start | bytes 147460
  432.0 18.1 %copy-start.31 = (f32[1,3,1,32,128]{4,3,2,1,0:T(8,128)}, f32[1,3,1,32,128]{4,3,2,1,0:T(8,128)S(1)}, u32[]{:S(2)}) copy-start(f32[1,3,1,32,128]{4,3,2,1,0:T(8,128)S(1)} %collective-permute-done.12) | copy-start | bytes 147460
  432.0 17.5 %collective-permute-start.15 = (f32[1,3,10,1,128]{4,3,2,1,0:T(1,128)S(1)}, f32[1,3,10,1,128]{4,3,2,1,0:T(1,128)S(1)}, u32[]{:S(2)}, u32[]{:S(2)}) collective-permute-start(f32[1,3,10,1,128]{4,3,2,1,0:T(1,128)S(1)} %get-tuple-element.70), channel_id=1, source_target_pairs={{1,0},{2,1},{3,2},{4,3},{5,4},{6,5},{7,6},{8,7},{9,8},{10,9},{11,1... | collective-permute-start | bytes 46088 | tf_op jit(solution)/shard_map/ppermute | solution.py:18
  433.3 16.2 %collective-permute-start.14 = (f32[1,3,10,1,128]{4,3,2,1,0:T(1,128)S(1)}, f32[1,3,10,1,128]{4,3,2,1,0:T(1,128)S(1)}, u32[]{:S(2)}, u32[]{:S(2)}) collective-permute-start(f32[1,3,10,1,128]{4,3,2,1,0:T(1,128)S(1)} %get-tuple-element.69), channel_id=1, source_target_pairs={{0,1},{1,2},{2,3},{3,4},{4,5},{5,6},{6,7},{7,8},{8,9},{9,10},{10,1... | collective-permute-start | bytes 46088 | tf_op jit(solution)/shard_map/ppermute | solution.py:15
  438.1 23.9 %all-to-all-start.2 = ((f32[32,1,2,128]{3,2,1,0:T(2,128)}), f32[32,1,2,128]{3,2,1,0:T(2,128)}, u32[]{:S(2)}, u32[]{:S(2)}) async-start(f32[32,1,2,128]{3,2,1,0:T(2,128)} %stack.14), calls=%async_computation.2 | async-start | bytes 65536 | tf_op jit(solution)/shard_map/all_to_all | solution.py:68
  505.4 135.7 %copy-start.47 = (s32[2]{0:T(128)S(1)}, s32[2]{0:T(128)}, u32[]{:S(2)}) copy-start(s32[2]{0:T(128)} %param.22) | copy-start | bytes 28
  621.5 20.8 %copy-start.34 = (f32[1,3,8,32,128]{4,3,2,1,0:T(8,128)}, f32[1,3,8,32,128]{4,3,2,1,0:T(8,128)S(1)}, u32[]{:S(2)}) copy-start(f32[1,3,8,32,128]{4,3,2,1,0:T(8,128)S(1)} %multiply_add_fusion) | copy-start | bytes 1179652
  (35 other events, 79.2 us)
